TPU v7x, 32 devices: a whole 2x2x4 slice. The times are simulated.
32 devices in a mesh: ctx: 4 (over y, x), ch: 8 (over z, core).
Axes of the slice: x: 2, y: 2, z: 4, core: 2. Of those that a mesh axis runs over, the one named last changes fastest.
Arguments:
- queries: bfloat16 [4096, 4096], P('ctx', 'ch'), may hold values from -12 to 12
- key_input: bfloat16 [4096, 4096], P('ctx', 'ch'), may hold values from -6 to 6
- value_input: bfloat16 [4096, 4096], P('ctx', 'ch'), may hold values from -6 to 6
- filters: bfloat16 [4096, 4096], P('ctx', 'ch'), may hold values from -0.3 to 0.3
- skip_gain: float32 [4096], P('ch'), may hold values from -0.3 to 0.3
- out_weight: bfloat16 [4096, 4096], P('ch'), may hold values from -0.125 to 0.125
Outputs:
- layer_out: bfloat16 [4096, 4096], P('ctx', 'ch')
All inputs are finite; a program needn't handle non-finite values.
Results may differ from a plain program's by a relative error of at most 0.019.
Values may be sent and summed in bfloat16 or wider, within the bound.
A program may use at most 320 MiB of HBM per device.

v0:
```python
import jax
import jax.numpy as jnp
from jax import lax
from jax.sharding import PartitionSpec as P

outer_radix = 64


def shifted(block, axis, distance):
    devices = range(lax.axis_size(axis))
    route = [(i - distance, i) for i in devices if i - distance in devices]
    return lax.ppermute(block, axis, route)


def split_pieces(values):
    if values.dtype == jnp.bfloat16:
        return [(values, 0)]
    high_part = values.astype(jnp.bfloat16)
    low_part = (values - high_part.astype(jnp.float32)).astype(jnp.bfloat16)
    return [(high_part, 0), (low_part, 1)]


def split_dot(form, left, right):
    total = None
    for left_piece, left_order in split_pieces(left):
        for right_piece, right_order in split_pieces(right):
            if left_order + right_order <= 1:
                term = jnp.einsum(form, left_piece, right_piece, preferred_element_type=jnp.float32)
                total = term if total is None else total + term
    return total


def angle_table(rows, columns, period):
    row_index = jnp.arange(rows, dtype=jnp.int32)[:, None]
    col_index = jnp.arange(columns, dtype=jnp.int32)[None, :]
    phases = row_index * col_index % period
    angles = phases.astype(jnp.float32) * (2.0 * jnp.pi / period)
    return (jnp.cos(angles), jnp.sin(angles))


def forward(signal, length):
    inner_len = length // outer_radix
    used_rows = signal.shape[0] // inner_len
    columns = signal.shape[1]
    folded = signal.reshape(used_rows, inner_len, columns)
    cos_outer, sin_outer = angle_table(outer_radix, used_rows, outer_radix)
    first_real = split_dot("kn,nqc->kqc", cos_outer, folded)
    first_imag = -split_dot("kn,nqc->kqc", sin_outer, folded)
    cos_twist, sin_twist = angle_table(outer_radix, inner_len, length)
    cos_twist = cos_twist[:, :, None]
    sin_twist = sin_twist[:, :, None]
    twist_real = first_real * cos_twist + first_imag * sin_twist
    twist_imag = first_imag * cos_twist - first_real * sin_twist
    cos_inner, sin_inner = angle_table(inner_len, inner_len, inner_len)
    spec_real = split_dot("kqc,qm->kmc", twist_real, cos_inner) + split_dot(
        "kqc,qm->kmc", twist_imag, sin_inner
    )
    spec_imag = split_dot("kqc,qm->kmc", twist_imag, cos_inner) - split_dot(
        "kqc,qm->kmc", twist_real, sin_inner
    )
    return (spec_real, spec_imag)


def inverse_tail(spec_real, spec_imag, length):
    inner_len = length // outer_radix
    cos_inner, sin_inner = angle_table(inner_len, inner_len, inner_len)
    back_real = split_dot("kmc,mq->kqc", spec_real, cos_inner) - split_dot(
        "kmc,mq->kqc", spec_imag, sin_inner
    )
    back_imag = split_dot("kmc,mq->kqc", spec_imag, cos_inner) + split_dot(
        "kmc,mq->kqc", spec_real, sin_inner
    )
    cos_twist, sin_twist = angle_table(outer_radix, inner_len, length)
    cos_twist = cos_twist[:, :, None]
    sin_twist = sin_twist[:, :, None]
    turn_real = back_real * cos_twist - back_imag * sin_twist
    turn_imag = back_imag * cos_twist + back_real * sin_twist
    cos_outer, sin_outer = angle_table(outer_radix, outer_radix, outer_radix)
    half_rows = outer_radix // 2
    tail_rows = split_dot("nk,kqc->nqc", cos_outer[half_rows:], turn_real) - split_dot(
        "nk,kqc->nqc", sin_outer[half_rows:], turn_imag
    )
    return tail_rows.reshape(half_rows * inner_len, -1) / length


def cycle_conv(mixed_in, filters, length):
    tok_rows, channels = mixed_in.shape
    all_segments = lax.all_gather(filters, "ctx", axis=0, tiled=True)
    padded = jnp.concatenate(
        [jnp.zeros((tok_rows, channels), all_segments.dtype), all_segments], axis=0
    )

    def add_lag(lag_index, held_block, sum_real, sum_imag):
        window = lax.dynamic_slice_in_dim(padded, lag_index * tok_rows, length, 0)
        filter_real, filter_imag = forward(window, length)
        input_real, input_imag = forward(held_block, length)
        sum_real = sum_real + input_real * filter_real - input_imag * filter_imag
        sum_imag = sum_imag + input_real * filter_imag + input_imag * filter_real
        return (sum_real, sum_imag)

    ctx_count = lax.axis_size("ctx")
    empty_spec = jnp.zeros((outer_radix, length // outer_radix, channels), jnp.float32)

    def cycle_step(lag_index, cycle_state):
        held_block, sum_real, sum_imag = cycle_state
        sum_real, sum_imag = add_lag(lag_index, held_block, sum_real, sum_imag)
        held_block = shifted(held_block, "ctx", 1)
        return (held_block, sum_real, sum_imag)

    held_block, sum_real, sum_imag = lax.fori_loop(
        0, ctx_count - 1, cycle_step, (mixed_in, empty_spec, empty_spec)
    )
    sum_real, sum_imag = add_lag(ctx_count - 1, held_block, sum_real, sum_imag)
    return inverse_tail(sum_real, sum_imag, length)


def per_device(queries, key_input, value_input, filters, skip_gain, out_weight):
    tok_rows, channels = queries.shape
    length = 2 * tok_rows
    mixed_in = (key_input.astype(jnp.float32) * value_input.astype(jnp.float32)).astype(
        jnp.bfloat16
    )
    conv = cycle_conv(mixed_in, filters, length)
    gated = (
        queries.astype(jnp.float32) * (conv + skip_gain[None, :] * mixed_in.astype(jnp.float32))
    ).astype(jnp.bfloat16)
    shares = lax.psum_scatter(
        lax.dot_general(
            out_weight, gated, (((0,), (1,)), ((), ())), preferred_element_type=jnp.float32
        ).astype(jnp.bfloat16),
        "ch",
        scatter_dimension=0,
        tiled=True,
    ).astype(jnp.float32)
    return shares.T.astype(jnp.bfloat16)


def solution(mesh):
    in_specs = (
        P("ctx", "ch"),
        P("ctx", "ch"),
        P("ctx", "ch"),
        P("ctx", "ch"),
        P("ch"),
        P("ch", None),
    )
    out_specs = P("ctx", "ch")
    return jax.shard_map(
        per_device, mesh=mesh, in_specs=in_specs, out_specs=out_specs, check_vma=False
    )
```

profile of v0, /device:TPU:0, one launch (start us, length us, event | category | flops | bytes accessed | tf_op | source)
XLA Modules:
  0.0 963.6 jit_solution(6129385879402401914)
XLA Ops:
  13.3 51.3 %all-gather.2.cloned.1.call-done = bf16[4096,512]{1,0:T(8,128)(2,1)} async-done(((bf16[1024,512]{1,0:T(8,128)(2,1)}), bf16[4096,512]{1,0:T(8,128)(2,1)}) %all-gather.2.cloned.1.call-update) | async-done | bytes 4194320 | tf_op jit(solution)/shard_map/all_gather | solution.py:88
  69.5 523.9 %while.21 = (s32[]{:T(128)}, bf16[1024,512]{1,0:T(8,128)(2,1)}, f32[64,32,512]{2,1,0:T(8,128)}, f32[64,32,512]{2,1,0:T(8,128)}, bf16[5120,512]{1,0:T(8,128)(2,1)...) while((s32[]{:T(128)}, bf16[1024,512]{1,0:T(8,128)(2,1)}, f32[64,32,512]{2,1,0:T(8,128)}, ...), condition=%wide.region_1.2_spmd.clone, body=%wide.region_0.1_spmd.clone.sunk | while | flops 2483855360 | bytes 476086720 | solution.py:110
  98.7 11.0 %subtract_convert_fusion.35 = (bf16[64,32,512]{2,0,1:T(8,128)(2,1)}, bf16[64,32,512]{2,0,1:T(8,128)(2,1)S(1)}, bf16[64,32,512]{2,0,1:T(8,128)(2,1)S(1)}, bf16[64...) fusion(f32[64,32]{0,1:T(8,128)S(1)} %get-tuple-element.274, ...), kind=kOutput, calls=%fused_computation.9.clone.1 | convolution fusion | flops 165748736 | bytes 35667968 | tf_op jit(solution)/shard_map/while/body/eval_jaxpr/kn,nqc->kqc/dot_general | solution.py:28
  185.1 12.3 %add_subtract_fusion.5 = f32[32,64,512]{2,0,1:T(8,128)} fusion(f32[32,64,512]{2,0,1:T(8,128)} %fusion.866, f32[32,64,512]{2,0,1:T(8,128)} %fusion.867, f32[32,64,512]{2,0,1:T(8,128)} %fusion.868, f32[32,64,512]{2,0,1:T(8,128)} %fusion.869, f32[32,64,512]{2,0,1:T(8,128)} %fusion.870, bf16[64,32,512]{2,0,1:T(8,128)(2,1)} %get-tuple-element.277), kind=kOutput, calls=%fused_computation.4.clone.1 | convolution fusion | flops 72367104 | bytes 27262976 | tf_op jit(solution)/shard_map/while/body/eval_jaxpr/kqc,qm->kmc/dot_general | solution.py:28
  197.5 10.7 %add_add_fusion.7 = f32[32,64,512]{2,0,1:T(8,128)} fusion(f32[32,64,512]{2,0,1:T(8,128)S(1)} %copy-done.8, f32[32,64,512]{2,0,1:T(8,128)} %fusion.862, f32[32,64,512]{2,0,1:T(8,128)} %fusion.863, f32[32,64,512]{2,0,1:T(8,128)} %fusion.864, f32[32,64,512]{2,0,1:T(8,128)} %fusion.865, bf16[64,32,512]{2,0,1:T(8,128)(2,1)S(1)} %copy-done.1), kind=kOutput, calls=%fused_computation.12.clone.1 | convolution fusion | flops 72367104 | bytes 27262976 | tf_op jit(solution)/shard_map/while/body/eval_jaxpr/kqc,qm->kmc/dot_general | solution.py:28
  209.7 6.9 add_add_fusion.6
  216.6 17.4 %bitcast_add_fusion.8 = (f32[64,32,512]{2,1,0:T(8,128)}, f32[64,32,512]{2,1,0:T(8,128)}) fusion(f32[64,32,512]{2,1,0:T(8,128)} %get-tuple-element.298, f32[32,64,512]{2,0,1:T(8,128)} %add_add_fusion.6, f32[32,64,512]{2,0,1:T(8,128)} %add_add_fusion.7, f32[32,64,512]{2,0,1:T(8,128)} %add_subtract_fusion.5, pred[]{:T(512)S(6)} %compare.21, ...), kind=kOutput, calls=%fused_computation.clone.1 | convolution fusion | flops 82852864 | bytes 52428800 | tf_op jit(solution)/shard_map/while/body/eval_jaxpr/kqc,qm->kmc/dot_general | solution.py:28
  262.0 21.1 %subtract_convert_fusion.35 = (bf16[64,32,512]{2,0,1:T(8,128)(2,1)}, bf16[64,32,512]{2,0,1:T(8,128)(2,1)S(1)}, bf16[64,32,512]{2,0,1:T(8,128)(2,1)S(1)}, bf16[64...) fusion(f32[64,32]{0,1:T(8,128)S(1)} %get-tuple-element.274, ...), kind=kOutput, calls=%fused_computation.9.clone.1 | convolution fusion | flops 165748736 | bytes 35667968 | tf_op jit(solution)/shard_map/while/body/eval_jaxpr/kn,nqc->kqc/dot_general | solution.py:28
  358.5 12.3 %add_subtract_fusion.5 = f32[32,64,512]{2,0,1:T(8,128)} fusion(f32[32,64,512]{2,0,1:T(8,128)} %fusion.866, f32[32,64,512]{2,0,1:T(8,128)} %fusion.867, f32[32,64,512]{2,0,1:T(8,128)} %fusion.868, f32[32,64,512]{2,0,1:T(8,128)} %fusion.869, f32[32,64,512]{2,0,1:T(8,128)} %fusion.870, bf16[64,32,512]{2,0,1:T(8,128)(2,1)} %get-tuple-element.277), kind=kOutput, calls=%fused_computation.4.clone.1 | convolution fusion | flops 72367104 | bytes 27262976 | tf_op jit(solution)/shard_map/while/body/eval_jaxpr/kqc,qm->kmc/dot_general | solution.py:28
  370.9 10.7 %add_add_fusion.7 = f32[32,64,512]{2,0,1:T(8,128)} fusion(f32[32,64,512]{2,0,1:T(8,128)S(1)} %copy-done.8, f32[32,64,512]{2,0,1:T(8,128)} %fusion.862, f32[32,64,512]{2,0,1:T(8,128)} %fusion.863, f32[32,64,512]{2,0,1:T(8,128)} %fusion.864, f32[32,64,512]{2,0,1:T(8,128)} %fusion.865, bf16[64,32,512]{2,0,1:T(8,128)(2,1)S(1)} %copy-done.1), kind=kOutput, calls=%fused_computation.12.clone.1 | convolution fusion | flops 72367104 | bytes 27262976 | tf_op jit(solution)/shard_map/while/body/eval_jaxpr/kqc,qm->kmc/dot_general | solution.py:28
  383.1 6.9 add_add_fusion.6
  390.0 19.8 %bitcast_add_fusion.8 = (f32[64,32,512]{2,1,0:T(8,128)}, f32[64,32,512]{2,1,0:T(8,128)}) fusion(f32[64,32,512]{2,1,0:T(8,128)} %get-tuple-element.298, f32[32,64,512]{2,0,1:T(8,128)} %add_add_fusion.6, f32[32,64,512]{2,0,1:T(8,128)} %add_add_fusion.7, f32[32,64,512]{2,0,1:T(8,128)} %add_subtract_fusion.5, pred[]{:T(512)S(6)} %compare.21, ...), kind=kOutput, calls=%fused_computation.clone.1 | convolution fusion | flops 82852864 | bytes 52428800 | tf_op jit(solution)/shard_map/while/body/eval_jaxpr/kqc,qm->kmc/dot_general | solution.py:28
  437.0 21.1 %subtract_convert_fusion.35 = (bf16[64,32,512]{2,0,1:T(8,128)(2,1)}, bf16[64,32,512]{2,0,1:T(8,128)(2,1)S(1)}, bf16[64,32,512]{2,0,1:T(8,128)(2,1)S(1)}, bf16[64...) fusion(f32[64,32]{0,1:T(8,128)S(1)} %get-tuple-element.274, ...), kind=kOutput, calls=%fused_computation.9.clone.1 | convolution fusion | flops 165748736 | bytes 35667968 | tf_op jit(solution)/shard_map/while/body/eval_jaxpr/kn,nqc->kqc/dot_general | solution.py:28
  533.5 12.3 %add_subtract_fusion.5 = f32[32,64,512]{2,0,1:T(8,128)} fusion(f32[32,64,512]{2,0,1:T(8,128)} %fusion.866, f32[32,64,512]{2,0,1:T(8,128)} %fusion.867, f32[32,64,512]{2,0,1:T(8,128)} %fusion.868, f32[32,64,512]{2,0,1:T(8,128)} %fusion.869, f32[32,64,512]{2,0,1:T(8,128)} %fusion.870, bf16[64,32,512]{2,0,1:T(8,128)(2,1)} %get-tuple-element.277), kind=kOutput, calls=%fused_computation.4.clone.1 | convolution fusion | flops 72367104 | bytes 27262976 | tf_op jit(solution)/shard_map/while/body/eval_jaxpr/kqc,qm->kmc/dot_general | solution.py:28
  545.9 10.7 %add_add_fusion.7 = f32[32,64,512]{2,0,1:T(8,128)} fusion(f32[32,64,512]{2,0,1:T(8,128)S(1)} %copy-done.8, f32[32,64,512]{2,0,1:T(8,128)} %fusion.862, f32[32,64,512]{2,0,1:T(8,128)} %fusion.863, f32[32,64,512]{2,0,1:T(8,128)} %fusion.864, f32[32,64,512]{2,0,1:T(8,128)} %fusion.865, bf16[64,32,512]{2,0,1:T(8,128)(2,1)S(1)} %copy-done.1), kind=kOutput, calls=%fused_computation.12.clone.1 | convolution fusion | flops 72367104 | bytes 27262976 | tf_op jit(solution)/shard_map/while/body/eval_jaxpr/kqc,qm->kmc/dot_general | solution.py:28
  558.1 6.9 add_add_fusion.6
  564.9 19.8 %bitcast_add_fusion.8 = (f32[64,32,512]{2,1,0:T(8,128)}, f32[64,32,512]{2,1,0:T(8,128)}) fusion(f32[64,32,512]{2,1,0:T(8,128)} %get-tuple-element.298, f32[32,64,512]{2,0,1:T(8,128)} %add_add_fusion.6, f32[32,64,512]{2,0,1:T(8,128)} %add_add_fusion.7, f32[32,64,512]{2,0,1:T(8,128)} %add_subtract_fusion.5, pred[]{:T(512)S(6)} %compare.21, ...), kind=kOutput, calls=%fused_computation.clone.1 | convolution fusion | flops 82852864 | bytes 52428800 | tf_op jit(solution)/shard_map/while/body/eval_jaxpr/kqc,qm->kmc/dot_general | solution.py:28
  619.8 11.0 %subtract_convert_fusion.15 = (bf16[64,32,512]{2,0,1:T(8,128)(2,1)}, bf16[64,32,512]{2,0,1:T(8,128)(2,1)S(1)}, bf16[64,32,512]{2,0,1:T(8,128)(2,1)S(1)}, bf16[64...) fusion(f32[64,32]{0,1:T(8,128)S(1)} %copy-done.23, ...), kind=kOutput, calls=%fused_computation.320 | convolution fusion | flops 165748736 | bytes 35667968 | tf_op jit(solution)/shard_map/kn,nqc->kqc/dot_general | solution.py:28
  702.1 9.2 add_subtract_fusion.2
  711.3 11.7 %add_add_fusion.3 = f32[32,64,512]{2,0,1:T(8,128)} fusion(f32[32,64,512]{2,0,1:T(8,128)} %fusion.339, f32[32,64,512]{2,0,1:T(8,128)} %fusion.337, f32[32,64,512]{2,0,1:T(8,128)} %fusion.309, f32[32,64,512]{2,0,1:T(8,128)} %fusion.347, f32[32,64,512]{2,0,1:T(8,128)} %fusion.345, bf16[64,32,512]{2,0,1:T(8,128)(2,1)S(1)} %copy-done.13), kind=kOutput, calls=%fused_computation.323 | convolution fusion | flops 72367104 | bytes 27262976 | tf_op jit(solution)/shard_map/kqc,qm->kmc/dot_general | solution.py:28
  723.0 7.1 add_add_fusion.2
  730.1 19.3 %bitcast_add_fusion.3 = (f32[64,32,512]{2,1,0:T(8,128)}, f32[64,32,512]{2,1,0:T(8,128)}) fusion(f32[64,32,512]{2,1,0:T(8,128)} %get-tuple-element.167, f32[32,64,512]{2,0,1:T(8,128)} %add_add_fusion.2, f32[32,64,512]{2,0,1:T(8,128)} %add_add_fusion.3, f32[32,64,512]{2,0,1:T(8,128)} %add_subtract_fusion.2, f32[64,32,512]{2,1,0:T(8,128)} %get-tuple-element.165, ...), kind=kOutput, calls=%fused_computation.297 | convolution fusion | flops 80755712 | bytes 52428800 | tf_op jit(solution)/shard_map/kqc,qm->kmc/dot_general | solution.py:28
  787.0 59.6 %fusion.356 = (bf16[64,32,512]{2,0,1:T(8,128)(2,1)S(1)}, f32[32,64,512]{2,1,0:T(8,128)}, f32[32,64,512]{2,1,0:T(8,128)}) fusion(f32[64,32]{0,1:T(8,128)S(1)} %copy-done.23, f32[64,32]{0,1:T(8,128)S(1)} %copy-done.24, f32[32,64,512]{2,0,1:T(8,128)} %fusion.417, f32[32,64,512]{2,0,1:T(8,128)} %fusion.502, f32[32,64,512]{2,0,1:T(8,128)} %fusion.419, ...), kind=kLoop, calls=%fused_computation.393 | loop fusion | flops 14680064 | bytes 60833792 | tf_op jit(solution)/shard_map/convert_element_type | solution.py:18
  867.6 88.9 %reduce-scatter.2.cloned.1.call-done = bf16[512,1024]{0,1:T(8,128)(2,1)} async-done(((bf16[4096,1024]{0,1:T(8,128)(2,1)}), bf16[512,1024]{0,1:T(8,128)(2,1)}) %reduce-scatter.2.cloned.1.call-update) | async-done | bytes 1048592 | tf_op jit(solution)/shard_map/reduce_scatter | solution.py:127
  (252 shorter events, 481.6 us)
Async XLA Ops:
  6.5 58.1 %all-gather.2.cloned.1.call-start = ((), (), s32[]{:S(2)}) async-start(), calls=%async_computation.1 | async-start | bytes 5242880 | tf_op jit(solution)/shard_map/all_gather | solution.py:88
  7.3 949.3 %reduce-scatter.2.cloned.1.call-start = ((), (), s32[]{:S(2)}) async-start(), calls=%async_computation.2 | async-start | bytes 9437184 | tf_op jit(solution)/shard_map/reduce_scatter | solution.py:127
  71.2 162.8 %collective-permute-start = (bf16[1024,512]{1,0:T(8,128)(2,1)S(1)}, bf16[1024,512]{1,0:T(8,128)(2,1)}, u32[]{:S(2)}, u32[]{:S(2)}) collective-permute-start(bf16[1024,512]{1,0:T(8,128)(2,1)S(1)} %copy.397), channel_id=1, source_target_pairs={{0,8},{8,16},{16,24},{1,9},{9,17},{17,25},{2,10},{10,18},{18,26},{... | collective-permute-start | bytes 3145736 | tf_op jit(solution)/shard_map/while/body/eval_jaxpr/ppermute | solution.py:12
  185.1 12.4 %copy-start.1 = (bf16[64,32,512]{2,0,1:T(8,128)(2,1)S(1)}, bf16[64,32,512]{2,0,1:T(8,128)(2,1)}, u32[]{:S(2)}) copy-start(bf16[64,32,512]{2,0,1:T(8,128)(2,1)} %get-tuple-element.283) | copy-start | bytes 6291460 | tf_op jit(solution)/shard_map/while
  185.1 12.4 %copy-start.8 = (f32[32,64,512]{2,0,1:T(8,128)S(1)}, f32[32,64,512]{2,0,1:T(8,128)}, u32[]{:S(2)}) copy-start(f32[32,64,512]{2,0,1:T(8,128)} %fusion.861) | copy-start | bytes 12582916 | tf_op jit(solution)/shard_map/while
  197.5 10.7 %copy-start.4 = (f32[32,64,512]{2,0,1:T(8,128)S(1)}, f32[32,64,512]{2,0,1:T(8,128)}, u32[]{:S(2)}) copy-start(f32[32,64,512]{2,0,1:T(8,128)} %fusion.856) | copy-start | bytes 12582916 | tf_op jit(solution)/shard_map/while
  197.5 10.7 %copy-start.5 = (f32[32,64,512]{2,0,1:T(8,128)S(1)}, f32[32,64,512]{2,0,1:T(8,128)}, u32[]{:S(2)}) copy-start(f32[32,64,512]{2,0,1:T(8,128)} %fusion.857) | copy-start | bytes 12582916 | tf_op jit(solution)/shard_map/while
  197.5 10.7 %copy-start.6 = (f32[32,64,512]{2,0,1:T(8,128)S(1)}, f32[32,64,512]{2,0,1:T(8,128)}, u32[]{:S(2)}) copy-start(f32[32,64,512]{2,0,1:T(8,128)} %fusion.859) | copy-start | bytes 12582916 | tf_op jit(solution)/shard_map/while
  197.5 12.2 %copy-start.7 = (f32[32,64,512]{2,0,1:T(8,128)S(1)}, f32[32,64,512]{2,0,1:T(8,128)}, u32[]{:S(2)}) copy-start(f32[32,64,512]{2,0,1:T(8,128)} %fusion.860) | copy-start | bytes 12582916 | tf_op jit(solution)/shard_map/while
  235.5 174.3 %collective-permute-start = (bf16[1024,512]{1,0:T(8,128)(2,1)S(1)}, bf16[1024,512]{1,0:T(8,128)(2,1)}, u32[]{:S(2)}, u32[]{:S(2)}) collective-permute-start(bf16[1024,512]{1,0:T(8,128)(2,1)S(1)} %copy.397), channel_id=1, source_target_pairs={{0,8},{8,16},{16,24},{1,9},{9,17},{17,25},{2,10},{10,18},{18,26},{... | collective-permute-start | bytes 3145736 | tf_op jit(solution)/shard_map/while/body/eval_jaxpr/ppermute | solution.py:12
  358.5 12.4 %copy-start.1 = (bf16[64,32,512]{2,0,1:T(8,128)(2,1)S(1)}, bf16[64,32,512]{2,0,1:T(8,128)(2,1)}, u32[]{:S(2)}) copy-start(bf16[64,32,512]{2,0,1:T(8,128)(2,1)} %get-tuple-element.283) | copy-start | bytes 6291460 | tf_op jit(solution)/shard_map/while
  358.5 12.4 %copy-start.8 = (f32[32,64,512]{2,0,1:T(8,128)S(1)}, f32[32,64,512]{2,0,1:T(8,128)}, u32[]{:S(2)}) copy-start(f32[32,64,512]{2,0,1:T(8,128)} %fusion.861) | copy-start | bytes 12582916 | tf_op jit(solution)/shard_map/while
  370.9 10.7 %copy-start.4 = (f32[32,64,512]{2,0,1:T(8,128)S(1)}, f32[32,64,512]{2,0,1:T(8,128)}, u32[]{:S(2)}) copy-start(f32[32,64,512]{2,0,1:T(8,128)} %fusion.856) | copy-start | bytes 12582916 | tf_op jit(solution)/shard_map/while
  370.9 10.7 %copy-start.5 = (f32[32,64,512]{2,0,1:T(8,128)S(1)}, f32[32,64,512]{2,0,1:T(8,128)}, u32[]{:S(2)}) copy-start(f32[32,64,512]{2,0,1:T(8,128)} %fusion.857) | copy-start | bytes 12582916 | tf_op jit(solution)/shard_map/while
  370.9 12.2 %copy-start.7 = (f32[32,64,512]{2,0,1:T(8,128)S(1)}, f32[32,64,512]{2,0,1:T(8,128)}, u32[]{:S(2)}) copy-start(f32[32,64,512]{2,0,1:T(8,128)} %fusion.860) | copy-start | bytes 12582916 | tf_op jit(solution)/shard_map/while
  411.4 173.4 %collective-permute-start = (bf16[1024,512]{1,0:T(8,128)(2,1)S(1)}, bf16[1024,512]{1,0:T(8,128)(2,1)}, u32[]{:S(2)}, u32[]{:S(2)}) collective-permute-start(bf16[1024,512]{1,0:T(8,128)(2,1)S(1)} %copy.397), channel_id=1, source_target_pairs={{0,8},{8,16},{16,24},{1,9},{9,17},{17,25},{2,10},{10,18},{18,26},{... | collective-permute-start | bytes 3145736 | tf_op jit(solution)/shard_map/while/body/eval_jaxpr/ppermute | solution.py:12
  533.5 12.4 %copy-start.1 = (bf16[64,32,512]{2,0,1:T(8,128)(2,1)S(1)}, bf16[64,32,512]{2,0,1:T(8,128)(2,1)}, u32[]{:S(2)}) copy-start(bf16[64,32,512]{2,0,1:T(8,128)(2,1)} %get-tuple-element.283) | copy-start | bytes 6291460 | tf_op jit(solution)/shard_map/while
  533.5 12.4 %copy-start.8 = (f32[32,64,512]{2,0,1:T(8,128)S(1)}, f32[32,64,512]{2,0,1:T(8,128)}, u32[]{:S(2)}) copy-start(f32[32,64,512]{2,0,1:T(8,128)} %fusion.861) | copy-start | bytes 12582916 | tf_op jit(solution)/shard_map/while
  545.8 10.7 %copy-start.4 = (f32[32,64,512]{2,0,1:T(8,128)S(1)}, f32[32,64,512]{2,0,1:T(8,128)}, u32[]{:S(2)}) copy-start(f32[32,64,512]{2,0,1:T(8,128)} %fusion.856) | copy-start | bytes 12582916 | tf_op jit(solution)/shard_map/while
  545.8 10.7 %copy-start.5 = (f32[32,64,512]{2,0,1:T(8,128)S(1)}, f32[32,64,512]{2,0,1:T(8,128)}, u32[]{:S(2)}) copy-start(f32[32,64,512]{2,0,1:T(8,128)} %fusion.857) | copy-start | bytes 12582916 | tf_op jit(solution)/shard_map/while
  545.9 10.7 %copy-start.6 = (f32[32,64,512]{2,0,1:T(8,128)S(1)}, f32[32,64,512]{2,0,1:T(8,128)}, u32[]{:S(2)}) copy-start(f32[32,64,512]{2,0,1:T(8,128)} %fusion.859) | copy-start | bytes 12582916 | tf_op jit(solution)/shard_map/while
  545.9 12.2 %copy-start.7 = (f32[32,64,512]{2,0,1:T(8,128)S(1)}, f32[32,64,512]{2,0,1:T(8,128)}, u32[]{:S(2)}) copy-start(f32[32,64,512]{2,0,1:T(8,128)} %fusion.860) | copy-start | bytes 12582916 | tf_op jit(solution)/shard_map/while
  711.3 11.7 %copy-start.15 = (f32[32,64,512]{2,0,1:T(8,128)S(1)}, f32[32,64,512]{2,0,1:T(8,128)}, u32[]{:S(2)}) copy-start(f32[32,64,512]{2,0,1:T(8,128)} %fusion.317) | copy-start | bytes 12582916
  711.3 11.7 %copy-start.16 = (f32[32,64,512]{2,0,1:T(8,128)S(1)}, f32[32,64,512]{2,0,1:T(8,128)}, u32[]{:S(2)}) copy-start(f32[32,64,512]{2,0,1:T(8,128)} %fusion.325) | copy-start | bytes 12582916
  (28 other events, 109.4 us)
Sparse Core Ops, SparseCore 0:
  9.2 55.3 all-gather.1
  867.8 88.6 reduce-scatter.1
where the time goes:
time: 966 us; the launch traced here: 964 us
  matrix products  694 us (72%)
  waiting for transfers between devices  141 us (15%)
  other arithmetic  68.2 us (7%)
  local copies, waits for them, and re-layouts  26 us (3%)
  between operations  13.9 us (1%)
  starting transfers between devices  10.3 us (1%)
  loops' own time  10 us (1%)
    dot_general x146, matrix products, split_dot(): jnp.einsum(form, left_piece, right_piece, preferred_element_type=jnp.floa...  688 us
    reduce_scatter x1, waiting for transfers between devices, per_device(): lax.psum_scatter(lax.dot_general(out_weight, gated, (((0,), (1,)), ((), (...  88.9 us
    convert_element_type x2, other arithmetic, split_pieces(): high_part = values.astype(jnp.bfloat16)  63.5 us
    all_gather x1, waiting for transfers between devices, cycle_conv(): all_segments = lax.all_gather(filters, 'ctx', axis=0, tiled=True)  51.3 us
  transfers between devices with their start and end apart: 5, of which 2 were waited for; matrix products, arithmetic and copies ran while one was open for 52% of the time, Pallas kernels for 0%

commit v1 on v0

--- a/solution.py
+++ b/solution.py
@@ -85,7 +85,13 @@
 
 def cycle_conv(mixed_in, filters, length):
     tok_rows, channels = mixed_in.shape
-    all_segments = lax.all_gather(filters, "ctx", axis=0, tiled=True)
+    size = lax.axis_size("ctx")
+    held, blocks = (filters, [filters])
+    for _ in range(size - 1):
+        held = lax.ppermute(held, "ctx", [(i_2, (i_2 + 1) % size) for i_2 in range(size)])
+        blocks.insert(0, held)
+    line = jnp.concatenate(blocks, axis=0)
+    all_segments = jnp.roll(line, (lax.axis_index("ctx") + 1) * filters.shape[0], axis=0)
     padded = jnp.concatenate(
         [jnp.zeros((tok_rows, channels), all_segments.dtype), all_segments], axis=0
     )

time: 966 us -> 981 us (1.016)
  waiting for transfers between devices: 141 us -> 156 us
    ppermute x0 -> x3, waiting for transfers between devices: none -> 67.2 us  [cycle_conv(): lax.ppermute(held, 'ctx', [(i_2, (i_2 + 1) % size) for i_2 in range(size)])]
    all_gather x1 -> x0, waiting for transfers between devices: 51.3 us -> none  [cycle_conv(): all_segments = lax.all_gather(filters, 'ctx', axis=0, tiled=True)]
  transfers between devices with their start and end apart: 5 -> 7, of which waited for: 2 -> 4; matrix products, arithmetic and copies ran while one was open for 52% -> 49% of each run, Pallas kernels for 0% -> 0%
where the time goes in v1:
time: 981 us; the launch traced here: 978 us
  matrix products  685 us (70%)
  waiting for transfers between devices  156 us (16%)
  other arithmetic  68.2 us (7%)
  local copies, waits for them, and re-layouts  31.7 us (3%)
  between operations  13.9 us (1%)
  starting transfers between devices  13.4 us (1%)
    dot_general x146, matrix products, split_dot(): jnp.einsum(form, left_piece, right_piece, preferred_element_type=jnp.floa...  678 us
    reduce_scatter x1, waiting for transfers between devices, per_device(): lax.psum_scatter(lax.dot_general(out_weight, gated, (((0,), (1,)), ((), (...  89.1 us
    ppermute x3, waiting for transfers between devices, cycle_conv(): lax.ppermute(held, 'ctx', [(i_2, (i_2 + 1) % size) for i_2 in range(size)])  67.2 us
    convert_element_type x2, other arithmetic, split_pieces(): high_part = values.astype(jnp.bfloat16)  63.5 us
  transfers between devices with their start and end apart: 7, of which 4 were waited for; matrix products, arithmetic and copies ran while one was open for 49% of the time, Pallas kernels for 0%

profile of v1, /device:TPU:0, one launch (start us, length us, event | category | flops | bytes accessed | tf_op | source)
XLA Modules:
  0.0 977.9 jit_solution(11011523382794742809)
XLA Ops:
  9.5 24.3 %collective-permute-done.1 = bf16[1024,512]{1,0:T(8,128)(2,1)S(1)} collective-permute-done((bf16[1024,512]{1,0:T(8,128)(2,1)}, bf16[1024,512]{1,0:T(8,128)(2,1)S(1)}, u32[]{:S(2)}, u32[]{:S(2)}) %collective-permute-start.1) | collective-permute-done | bytes 1048608 | tf_op jit(solution)/shard_map/ppermute | solution.py:91
  34.6 24.5 %collective-permute-done.2 = bf16[1024,512]{1,0:T(8,128)(2,1)S(1)} collective-permute-done((bf16[1024,512]{1,0:T(8,128)(2,1)S(1)}, bf16[1024,512]{1,0:T(8,128)(2,1)S(1)}, u32[]{:S(2)}, u32[]{:S(2)}) %collective-permute-start.2) | collective-permute-done | bytes 1048608 | tf_op jit(solution)/shard_map/ppermute | solution.py:91
  65.1 18.4 %collective-permute-done.3 = bf16[1024,512]{1,0:T(8,128)(2,1)} collective-permute-done((bf16[1024,512]{1,0:T(8,128)(2,1)S(1)}, bf16[1024,512]{1,0:T(8,128)(2,1)}, u32[]{:S(2)}, u32[]{:S(2)}) %collective-permute-start.3) | collective-permute-done | bytes 1048608 | tf_op jit(solution)/shard_map/ppermute | solution.py:91
  92.5 503.1 %while.21 = (s32[]{:T(128)}, bf16[1024,512]{1,0:T(8,128)(2,1)}, f32[64,32,512]{2,1,0:T(8,128)}, f32[64,32,512]{2,1,0:T(8,128)}, bf16[5120,512]{1,0:T(8,128)(2,1)...) while((s32[]{:T(128)}, bf16[1024,512]{1,0:T(8,128)(2,1)}, f32[64,32,512]{2,1,0:T(8,128)}, ...), condition=%wide.region_1.2_spmd.clone, body=%wide.region_0.1_spmd.clone.sunk | while | flops 2483855360 | bytes 476086720 | solution.py:116
  119.3 11.3 %subtract_convert_fusion.35 = (bf16[64,32,512]{2,0,1:T(8,128)(2,1)}, bf16[64,32,512]{2,0,1:T(8,128)(2,1)S(1)}, bf16[64,32,512]{2,0,1:T(8,128)(2,1)S(1)}, bf16[64...) fusion(f32[64,32]{0,1:T(8,128)S(1)} %get-tuple-element.274, ...), kind=kOutput, calls=%fused_computation.9.clone.1 | convolution fusion | flops 165748736 | bytes 35667968 | tf_op jit(solution)/shard_map/while/body/eval_jaxpr/kn,nqc->kqc/dot_general | solution.py:28
  205.8 12.4 %add_subtract_fusion.5 = f32[32,64,512]{2,0,1:T(8,128)} fusion(f32[32,64,512]{2,0,1:T(8,128)} %fusion.866, f32[32,64,512]{2,0,1:T(8,128)} %fusion.867, f32[32,64,512]{2,0,1:T(8,128)} %fusion.868, f32[32,64,512]{2,0,1:T(8,128)} %fusion.869, f32[32,64,512]{2,0,1:T(8,128)} %fusion.870, bf16[64,32,512]{2,0,1:T(8,128)(2,1)} %get-tuple-element.277), kind=kOutput, calls=%fused_computation.4.clone.1 | convolution fusion | flops 72367104 | bytes 27262976 | tf_op jit(solution)/shard_map/while/body/eval_jaxpr/kqc,qm->kmc/dot_general | solution.py:28
  218.2 10.7 %add_add_fusion.7 = f32[32,64,512]{2,0,1:T(8,128)} fusion(f32[32,64,512]{2,0,1:T(8,128)S(1)} %copy-done.8, f32[32,64,512]{2,0,1:T(8,128)} %fusion.862, f32[32,64,512]{2,0,1:T(8,128)} %fusion.863, f32[32,64,512]{2,0,1:T(8,128)} %fusion.864, f32[32,64,512]{2,0,1:T(8,128)} %fusion.865, bf16[64,32,512]{2,0,1:T(8,128)(2,1)S(1)} %copy-done.1), kind=kOutput, calls=%fused_computation.12.clone.1 | convolution fusion | flops 72367104 | bytes 27262976 | tf_op jit(solution)/shard_map/while/body/eval_jaxpr/kqc,qm->kmc/dot_general | solution.py:28
  237.1 17.7 %bitcast_add_fusion.8 = (f32[64,32,512]{2,1,0:T(8,128)}, f32[64,32,512]{2,1,0:T(8,128)}) fusion(f32[64,32,512]{2,1,0:T(8,128)} %get-tuple-element.298, f32[32,64,512]{2,0,1:T(8,128)} %add_add_fusion.6, f32[32,64,512]{2,0,1:T(8,128)} %add_add_fusion.7, f32[32,64,512]{2,0,1:T(8,128)} %add_subtract_fusion.5, pred[]{:T(512)S(6)} %compare.22, ...), kind=kOutput, calls=%fused_computation.clone.1 | convolution fusion | flops 82852864 | bytes 52428800 | tf_op jit(solution)/shard_map/while/body/eval_jaxpr/kqc,qm->kmc/dot_general | solution.py:28
  284.5 11.3 %subtract_convert_fusion.35 = (bf16[64,32,512]{2,0,1:T(8,128)(2,1)}, bf16[64,32,512]{2,0,1:T(8,128)(2,1)S(1)}, bf16[64,32,512]{2,0,1:T(8,128)(2,1)S(1)}, bf16[64...) fusion(f32[64,32]{0,1:T(8,128)S(1)} %get-tuple-element.274, ...), kind=kOutput, calls=%fused_computation.9.clone.1 | convolution fusion | flops 165748736 | bytes 35667968 | tf_op jit(solution)/shard_map/while/body/eval_jaxpr/kn,nqc->kqc/dot_general | solution.py:28
  370.9 12.4 %add_subtract_fusion.5 = f32[32,64,512]{2,0,1:T(8,128)} fusion(f32[32,64,512]{2,0,1:T(8,128)} %fusion.866, f32[32,64,512]{2,0,1:T(8,128)} %fusion.867, f32[32,64,512]{2,0,1:T(8,128)} %fusion.868, f32[32,64,512]{2,0,1:T(8,128)} %fusion.869, f32[32,64,512]{2,0,1:T(8,128)} %fusion.870, bf16[64,32,512]{2,0,1:T(8,128)(2,1)} %get-tuple-element.277), kind=kOutput, calls=%fused_computation.4.clone.1 | convolution fusion | flops 72367104 | bytes 27262976 | tf_op jit(solution)/shard_map/while/body/eval_jaxpr/kqc,qm->kmc/dot_general | solution.py:28
  383.4 10.7 %add_add_fusion.7 = f32[32,64,512]{2,0,1:T(8,128)} fusion(f32[32,64,512]{2,0,1:T(8,128)S(1)} %copy-done.8, f32[32,64,512]{2,0,1:T(8,128)} %fusion.862, f32[32,64,512]{2,0,1:T(8,128)} %fusion.863, f32[32,64,512]{2,0,1:T(8,128)} %fusion.864, f32[32,64,512]{2,0,1:T(8,128)} %fusion.865, bf16[64,32,512]{2,0,1:T(8,128)(2,1)S(1)} %copy-done.1), kind=kOutput, calls=%fused_computation.12.clone.1 | convolution fusion | flops 72367104 | bytes 27262976 | tf_op jit(solution)/shard_map/while/body/eval_jaxpr/kqc,qm->kmc/dot_general | solution.py:28
  402.3 20.1 %bitcast_add_fusion.8 = (f32[64,32,512]{2,1,0:T(8,128)}, f32[64,32,512]{2,1,0:T(8,128)}) fusion(f32[64,32,512]{2,1,0:T(8,128)} %get-tuple-element.298, f32[32,64,512]{2,0,1:T(8,128)} %add_add_fusion.6, f32[32,64,512]{2,0,1:T(8,128)} %add_add_fusion.7, f32[32,64,512]{2,0,1:T(8,128)} %add_subtract_fusion.5, pred[]{:T(512)S(6)} %compare.22, ...), kind=kOutput, calls=%fused_computation.clone.1 | convolution fusion | flops 82852864 | bytes 52428800 | tf_op jit(solution)/shard_map/while/body/eval_jaxpr/kqc,qm->kmc/dot_general | solution.py:28
  449.2 11.3 %subtract_convert_fusion.35 = (bf16[64,32,512]{2,0,1:T(8,128)(2,1)}, bf16[64,32,512]{2,0,1:T(8,128)(2,1)S(1)}, bf16[64,32,512]{2,0,1:T(8,128)(2,1)S(1)}, bf16[64...) fusion(f32[64,32]{0,1:T(8,128)S(1)} %get-tuple-element.274, ...), kind=kOutput, calls=%fused_computation.9.clone.1 | convolution fusion | flops 165748736 | bytes 35667968 | tf_op jit(solution)/shard_map/while/body/eval_jaxpr/kn,nqc->kqc/dot_general | solution.py:28
  535.7 12.4 %add_subtract_fusion.5 = f32[32,64,512]{2,0,1:T(8,128)} fusion(f32[32,64,512]{2,0,1:T(8,128)} %fusion.866, f32[32,64,512]{2,0,1:T(8,128)} %fusion.867, f32[32,64,512]{2,0,1:T(8,128)} %fusion.868, f32[32,64,512]{2,0,1:T(8,128)} %fusion.869, f32[32,64,512]{2,0,1:T(8,128)} %fusion.870, bf16[64,32,512]{2,0,1:T(8,128)(2,1)} %get-tuple-element.277), kind=kOutput, calls=%fused_computation.4.clone.1 | convolution fusion | flops 72367104 | bytes 27262976 | tf_op jit(solution)/shard_map/while/body/eval_jaxpr/kqc,qm->kmc/dot_general | solution.py:28
  548.1 10.7 %add_add_fusion.7 = f32[32,64,512]{2,0,1:T(8,128)} fusion(f32[32,64,512]{2,0,1:T(8,128)S(1)} %copy-done.8, f32[32,64,512]{2,0,1:T(8,128)} %fusion.862, f32[32,64,512]{2,0,1:T(8,128)} %fusion.863, f32[32,64,512]{2,0,1:T(8,128)} %fusion.864, f32[32,64,512]{2,0,1:T(8,128)} %fusion.865, bf16[64,32,512]{2,0,1:T(8,128)(2,1)S(1)} %copy-done.1), kind=kOutput, calls=%fused_computation.12.clone.1 | convolution fusion | flops 72367104 | bytes 27262976 | tf_op jit(solution)/shard_map/while/body/eval_jaxpr/kqc,qm->kmc/dot_general | solution.py:28
  567.0 20.1 %bitcast_add_fusion.8 = (f32[64,32,512]{2,1,0:T(8,128)}, f32[64,32,512]{2,1,0:T(8,128)}) fusion(f32[64,32,512]{2,1,0:T(8,128)} %get-tuple-element.298, f32[32,64,512]{2,0,1:T(8,128)} %add_add_fusion.6, f32[32,64,512]{2,0,1:T(8,128)} %add_add_fusion.7, f32[32,64,512]{2,0,1:T(8,128)} %add_subtract_fusion.5, pred[]{:T(512)S(6)} %compare.22, ...), kind=kOutput, calls=%fused_computation.clone.1 | convolution fusion | flops 82852864 | bytes 52428800 | tf_op jit(solution)/shard_map/while/body/eval_jaxpr/kqc,qm->kmc/dot_general | solution.py:28
  623.5 21.2 %subtract_convert_fusion.15 = (bf16[64,32,512]{2,0,1:T(8,128)(2,1)}, bf16[64,32,512]{2,0,1:T(8,128)(2,1)S(1)}, bf16[64,32,512]{2,0,1:T(8,128)(2,1)S(1)}, bf16[64...) fusion(f32[64,32]{0,1:T(8,128)S(1)} %copy-done.24, ...), kind=kOutput, calls=%fused_computation.320 | convolution fusion | flops 165748736 | bytes 35667968 | tf_op jit(solution)/shard_map/kn,nqc->kqc/dot_general | solution.py:28
  716.2 9.2 add_subtract_fusion.2
  725.4 11.7 %add_add_fusion.3 = f32[32,64,512]{2,0,1:T(8,128)} fusion(f32[32,64,512]{2,0,1:T(8,128)} %fusion.339, f32[32,64,512]{2,0,1:T(8,128)} %fusion.337, f32[32,64,512]{2,0,1:T(8,128)} %fusion.309, f32[32,64,512]{2,0,1:T(8,128)} %fusion.347, f32[32,64,512]{2,0,1:T(8,128)} %fusion.345, bf16[64,32,512]{2,0,1:T(8,128)(2,1)S(1)} %copy-done.13), kind=kOutput, calls=%fused_computation.323 | convolution fusion | flops 72367104 | bytes 27262976 | tf_op jit(solution)/shard_map/kqc,qm->kmc/dot_general | solution.py:28
  737.1 7.1 add_add_fusion.2
  744.2 19.3 %bitcast_add_fusion.3 = (f32[64,32,512]{2,1,0:T(8,128)}, f32[64,32,512]{2,1,0:T(8,128)}) fusion(f32[64,32,512]{2,1,0:T(8,128)} %get-tuple-element.167, f32[32,64,512]{2,0,1:T(8,128)} %add_add_fusion.2, f32[32,64,512]{2,0,1:T(8,128)} %add_add_fusion.3, f32[32,64,512]{2,0,1:T(8,128)} %add_subtract_fusion.2, f32[64,32,512]{2,1,0:T(8,128)} %get-tuple-element.165, ...), kind=kOutput, calls=%fused_computation.297 | convolution fusion | flops 80755712 | bytes 52428800 | tf_op jit(solution)/shard_map/kqc,qm->kmc/dot_general | solution.py:28
  801.0 59.6 %fusion.356 = (bf16[64,32,512]{2,0,1:T(8,128)(2,1)S(1)}, f32[32,64,512]{2,1,0:T(8,128)}, f32[32,64,512]{2,1,0:T(8,128)}) fusion(f32[64,32]{0,1:T(8,128)S(1)} %copy-done.24, f32[64,32]{0,1:T(8,128)S(1)} %copy-done.25, f32[32,64,512]{2,0,1:T(8,128)} %fusion.417, f32[32,64,512]{2,0,1:T(8,128)} %fusion.502, f32[32,64,512]{2,0,1:T(8,128)} %fusion.419, ...), kind=kLoop, calls=%fused_computation.393 | loop fusion | flops 14680064 | bytes 60833792 | tf_op jit(solution)/shard_map/convert_element_type | solution.py:18
  874.8 6.9 convert_bitcast_fusion
  881.7 89.1 %reduce-scatter.2.cloned.1.call-done = bf16[512,1024]{0,1:T(8,128)(2,1)} async-done(((bf16[4096,1024]{0,1:T(8,128)(2,1)}), bf16[512,1024]{0,1:T(8,128)(2,1)}) %reduce-scatter.2.cloned.1.call-update) | async-done | bytes 1048592 | tf_op jit(solution)/shard_map/reduce_scatter | solution.py:133
  (266 shorter events, 502.4 us)
Async XLA Ops:
  6.5 964.3 %reduce-scatter.2.cloned.1.call-start = ((), (), s32[]{:S(2)}) async-start(), calls=%async_computation.1 | async-start | bytes 9437184 | tf_op jit(solution)/shard_map/reduce_scatter | solution.py:133
  6.5 27.3 %collective-permute-start.1 = (bf16[1024,512]{1,0:T(8,128)(2,1)}, bf16[1024,512]{1,0:T(8,128)(2,1)S(1)}, u32[]{:S(2)}, u32[]{:S(2)}) collective-permute-start(bf16[1024,512]{1,0:T(8,128)(2,1)} %param.11), channel_id=1, source_target_pairs={{0,8},{8,16},{16,24},{24,0},{1,9},{9,17},{17,25},{25,1},{2,10},{10... | collective-permute-start | bytes 3145736 | tf_op jit(solution)/shard_map/ppermute | solution.py:91
  33.8 25.2 %collective-permute-start.2 = (bf16[1024,512]{1,0:T(8,128)(2,1)S(1)}, bf16[1024,512]{1,0:T(8,128)(2,1)S(1)}, u32[]{:S(2)}, u32[]{:S(2)}) collective-permute-start(bf16[1024,512]{1,0:T(8,128)(2,1)S(1)} %collective-permute-done.1), channel_id=1, source_target_pairs={{0,8},{8,16},{16,24},{24,0},{1,9},{9,17},{17,25},{25,1},{2,10},{10... | collective-permute-start | bytes 3145736 | tf_op jit(solution)/shard_map/ppermute | solution.py:91
  59.0 24.4 %collective-permute-start.3 = (bf16[1024,512]{1,0:T(8,128)(2,1)S(1)}, bf16[1024,512]{1,0:T(8,128)(2,1)}, u32[]{:S(2)}, u32[]{:S(2)}) collective-permute-start(bf16[1024,512]{1,0:T(8,128)(2,1)S(1)} %collective-permute-done.2), channel_id=1, source_target_pairs={{0,8},{8,16},{16,24},{24,0},{1,9},{9,17},{17,25},{25,1},{2,10},{10... | collective-permute-start | bytes 3145736 | tf_op jit(solution)/shard_map/ppermute | solution.py:91
  61.9 23.1 %copy-start.22 = (bf16[1024,512]{1,0:T(8,128)(2,1)S(1)}, bf16[1024,512]{1,0:T(8,128)(2,1)}, u32[]{:S(2)}) copy-start(bf16[1024,512]{1,0:T(8,128)(2,1)} %param.11) | copy-start | bytes 3145732
  93.9 160.9 %collective-permute-start = (bf16[1024,512]{1,0:T(8,128)(2,1)S(1)}, bf16[1024,512]{1,0:T(8,128)(2,1)}, u32[]{:S(2)}, u32[]{:S(2)}) collective-permute-start(bf16[1024,512]{1,0:T(8,128)(2,1)S(1)} %copy.404), channel_id=1, source_target_pairs={{0,8},{8,16},{16,24},{1,9},{9,17},{17,25},{2,10},{10,18},{18,26},{... | collective-permute-start | bytes 3145736 | tf_op jit(solution)/shard_map/while/body/eval_jaxpr/ppermute | solution.py:12
  205.8 12.4 %copy-start.1 = (bf16[64,32,512]{2,0,1:T(8,128)(2,1)S(1)}, bf16[64,32,512]{2,0,1:T(8,128)(2,1)}, u32[]{:S(2)}) copy-start(bf16[64,32,512]{2,0,1:T(8,128)(2,1)} %get-tuple-element.283) | copy-start | bytes 6291460 | tf_op jit(solution)/shard_map/while
  205.8 12.4 %copy-start.8 = (f32[32,64,512]{2,0,1:T(8,128)S(1)}, f32[32,64,512]{2,0,1:T(8,128)}, u32[]{:S(2)}) copy-start(f32[32,64,512]{2,0,1:T(8,128)} %fusion.861) | copy-start | bytes 12582916 | tf_op jit(solution)/shard_map/while
  218.2 10.7 %copy-start.4 = (f32[32,64,512]{2,0,1:T(8,128)S(1)}, f32[32,64,512]{2,0,1:T(8,128)}, u32[]{:S(2)}) copy-start(f32[32,64,512]{2,0,1:T(8,128)} %fusion.856) | copy-start | bytes 12582916 | tf_op jit(solution)/shard_map/while
  218.2 10.7 %copy-start.5 = (f32[32,64,512]{2,0,1:T(8,128)S(1)}, f32[32,64,512]{2,0,1:T(8,128)}, u32[]{:S(2)}) copy-start(f32[32,64,512]{2,0,1:T(8,128)} %fusion.857) | copy-start | bytes 12582916 | tf_op jit(solution)/shard_map/while
  218.2 12.2 %copy-start.7 = (f32[32,64,512]{2,0,1:T(8,128)S(1)}, f32[32,64,512]{2,0,1:T(8,128)}, u32[]{:S(2)}) copy-start(f32[32,64,512]{2,0,1:T(8,128)} %fusion.860) | copy-start | bytes 12582916 | tf_op jit(solution)/shard_map/while
  256.3 166.1 %collective-permute-start = (bf16[1024,512]{1,0:T(8,128)(2,1)S(1)}, bf16[1024,512]{1,0:T(8,128)(2,1)}, u32[]{:S(2)}, u32[]{:S(2)}) collective-permute-start(bf16[1024,512]{1,0:T(8,128)(2,1)S(1)} %copy.404), channel_id=1, source_target_pairs={{0,8},{8,16},{16,24},{1,9},{9,17},{17,25},{2,10},{10,18},{18,26},{... | collective-permute-start | bytes 3145736 | tf_op jit(solution)/shard_map/while/body/eval_jaxpr/ppermute | solution.py:12
  370.9 12.4 %copy-start.1 = (bf16[64,32,512]{2,0,1:T(8,128)(2,1)S(1)}, bf16[64,32,512]{2,0,1:T(8,128)(2,1)}, u32[]{:S(2)}) copy-start(bf16[64,32,512]{2,0,1:T(8,128)(2,1)} %get-tuple-element.283) | copy-start | bytes 6291460 | tf_op jit(solution)/shard_map/while
  370.9 12.4 %copy-start.8 = (f32[32,64,512]{2,0,1:T(8,128)S(1)}, f32[32,64,512]{2,0,1:T(8,128)}, u32[]{:S(2)}) copy-start(f32[32,64,512]{2,0,1:T(8,128)} %fusion.861) | copy-start | bytes 12582916 | tf_op jit(solution)/shard_map/while
  383.3 10.7 %copy-start.4 = (f32[32,64,512]{2,0,1:T(8,128)S(1)}, f32[32,64,512]{2,0,1:T(8,128)}, u32[]{:S(2)}) copy-start(f32[32,64,512]{2,0,1:T(8,128)} %fusion.856) | copy-start | bytes 12582916 | tf_op jit(solution)/shard_map/while
  383.3 10.7 %copy-start.5 = (f32[32,64,512]{2,0,1:T(8,128)S(1)}, f32[32,64,512]{2,0,1:T(8,128)}, u32[]{:S(2)}) copy-start(f32[32,64,512]{2,0,1:T(8,128)} %fusion.857) | copy-start | bytes 12582916 | tf_op jit(solution)/shard_map/while
  383.4 12.2 %copy-start.7 = (f32[32,64,512]{2,0,1:T(8,128)S(1)}, f32[32,64,512]{2,0,1:T(8,128)}, u32[]{:S(2)}) copy-start(f32[32,64,512]{2,0,1:T(8,128)} %fusion.860) | copy-start | bytes 12582916 | tf_op jit(solution)/shard_map/while
  423.8 163.3 %collective-permute-start = (bf16[1024,512]{1,0:T(8,128)(2,1)S(1)}, bf16[1024,512]{1,0:T(8,128)(2,1)}, u32[]{:S(2)}, u32[]{:S(2)}) collective-permute-start(bf16[1024,512]{1,0:T(8,128)(2,1)S(1)} %copy.404), channel_id=1, source_target_pairs={{0,8},{8,16},{16,24},{1,9},{9,17},{17,25},{2,10},{10,18},{18,26},{... | collective-permute-start | bytes 3145736 | tf_op jit(solution)/shard_map/while/body/eval_jaxpr/ppermute | solution.py:12
  535.7 12.4 %copy-start.1 = (bf16[64,32,512]{2,0,1:T(8,128)(2,1)S(1)}, bf16[64,32,512]{2,0,1:T(8,128)(2,1)}, u32[]{:S(2)}) copy-start(bf16[64,32,512]{2,0,1:T(8,128)(2,1)} %get-tuple-element.283) | copy-start | bytes 6291460 | tf_op jit(solution)/shard_map/while
  535.7 12.4 %copy-start.8 = (f32[32,64,512]{2,0,1:T(8,128)S(1)}, f32[32,64,512]{2,0,1:T(8,128)}, u32[]{:S(2)}) copy-start(f32[32,64,512]{2,0,1:T(8,128)} %fusion.861) | copy-start | bytes 12582916 | tf_op jit(solution)/shard_map/while
  548.1 10.7 %copy-start.4 = (f32[32,64,512]{2,0,1:T(8,128)S(1)}, f32[32,64,512]{2,0,1:T(8,128)}, u32[]{:S(2)}) copy-start(f32[32,64,512]{2,0,1:T(8,128)} %fusion.856) | copy-start | bytes 12582916 | tf_op jit(solution)/shard_map/while
  548.1 12.2 %copy-start.7 = (f32[32,64,512]{2,0,1:T(8,128)S(1)}, f32[32,64,512]{2,0,1:T(8,128)}, u32[]{:S(2)}) copy-start(f32[32,64,512]{2,0,1:T(8,128)} %fusion.860) | copy-start | bytes 12582916 | tf_op jit(solution)/shard_map/while
  725.4 11.7 %copy-start.15 = (f32[32,64,512]{2,0,1:T(8,128)S(1)}, f32[32,64,512]{2,0,1:T(8,128)}, u32[]{:S(2)}) copy-start(f32[32,64,512]{2,0,1:T(8,128)} %fusion.317) | copy-start | bytes 12582916
  725.4 11.7 %copy-start.16 = (f32[32,64,512]{2,0,1:T(8,128)S(1)}, f32[32,64,512]{2,0,1:T(8,128)}, u32[]{:S(2)}) copy-start(f32[32,64,512]{2,0,1:T(8,128)} %fusion.325) | copy-start | bytes 12582916
  (31 other events, 139.8 us)
Sparse Core Ops, SparseCore 0:
  881.9 88.9 reduce-scatter.1
